TPU v7x, 32 devices: a whole 2x2x4 slice. The times are simulated.
32 devices in a mesh: groups: 2 (over y), mem: 4 (over x, core), tp: 4 (over z).
Axes of the slice: x: 2, y: 2, z: 4, core: 2. Of those that a mesh axis runs over, the one named last changes fastest.
Arguments:
- questions: bfloat16 [16, 32, 4096], P(('groups', 'mem'), None, 'tp'), parts along dimension 0
- memory: bfloat16 [512, 64, 4096], P(('groups', 'mem'), None, 'tp'), parts along dimension 0
- pass_ids: int32 [16, 10], P('groups'), parts along dimension 0, may hold values from 0 to 255, as said below
- pass_map: int32 [512], P('groups'), parts along dimension 0, may hold values from 0 to 255, as said below
- norm_gain: bfloat16 [1, 4096], P(None, 'tp'), may hold values from 0.25 to 1.75
- w_query: bfloat16 [4096, 4096], P(None, 'tp')
- w_key: bfloat16 [4096, 4096], P(None, 'tp')
- w_value: bfloat16 [4096, 4096], P(None, 'tp'), may hold values from -0.375 to 0.375
- w_out: bfloat16 [4096, 4096], P('tp'), may hold values from -0.1875 to 0.1875
Outputs:
- mixed: bfloat16 [16, 10, 96, 4096], P(('groups', 'mem'), None, None, 'tp'), parts along dimension 0
There are 2 independent parts, one for each index of `groups`. A program takes and returns all parts, laid end to end along the dimension named above; an argument that names none is the same for every part. Nothing has to cross between parts.
Inputs may be any that keep to these rules, and one draw needn't show every extreme that they name: `pass_ids`: each question lists 10 different passages; of the 20 passages listed by the questions of one index of mem, at most 10 are stored on any one index of mem (storage rows k * 64 to (k + 1) * 64 - 1 for index k), and exactly 10 on some index. Passage p is stored at row pass_map[p] of memory; each row holds one passage.
All inputs are finite; a program needn't handle non-finite values.
Results may differ from a plain program's by a relative error of at most 0.0048.
Values may be sent and summed in bfloat16 or wider, within the bound.
A program may use at most 192 MiB of HBM per device.

v0:
```python
import jax
import jax.numpy as jnp
from jax import lax
from jax.sharding import PartitionSpec as P

HDIM = 64
NPASS = 10
QLEN = 32
PLEN = 64


def pair_layout(flat, q_count, last_width):
    pass_part = flat[: q_count * NPASS * PLEN].reshape(q_count, NPASS, PLEN, last_width)
    ques_part = flat[q_count * NPASS * PLEN :].reshape(q_count, 1, QLEN, last_width)
    ques_part = jnp.broadcast_to(ques_part, (q_count, NPASS, QLEN, last_width))
    return jnp.concatenate([ques_part, pass_part], axis=2)


def local(questions, memory, pass_ids, pass_map, norm_gain, w_query, w_key, w_value, w_out):
    readers = lax.axis_size("mem")
    own_index = lax.axis_index("mem")
    q_count = questions.shape[0]
    feat_width = questions.shape[2]
    slot_count = memory.shape[0]
    stored = pass_map.shape[0]
    per_reader = q_count * NPASS
    matches = pass_ids[:, :, None] == jnp.arange(stored, dtype=jnp.int32)[None, None, :]
    location = jnp.sum(jnp.where(matches, pass_map[None, None, :], 0), axis=2).reshape(
        readers, per_reader
    )
    own_location = lax.dynamic_index_in_dim(location, own_index, 0, keepdims=False)
    position = jnp.arange(per_reader, dtype=jnp.int32)
    earlier = position[:, None] > position[None, :]
    capacity = min(per_reader, 2 * -(-per_reader // readers))
    owners = location // slot_count
    mine = owners == own_index
    rank_mine = jnp.sum((mine[:, None, :] & earlier[None, :, :]).astype(jnp.int32), axis=2)
    slot_ids = jnp.arange(capacity, dtype=jnp.int32)
    pick = mine[:, None, :] & (rank_mine[:, None, :] == slot_ids[None, :, None])
    filled = jnp.any(pick, axis=2)
    slot_rows = jnp.sum(jnp.where(pick, (location % slot_count)[:, None, :], 0), axis=2)
    picked = jnp.take(memory, slot_rows.reshape(-1), axis=0).reshape(
        readers, capacity, PLEN, feat_width
    )
    outgoing = jnp.where(filled[:, :, None, None], picked, jnp.zeros_like(picked))
    incoming = lax.all_to_all(outgoing, "mem", split_axis=0, concat_axis=0, tiled=True)
    sources = own_location // slot_count
    same_source = sources[:, None] == sources[None, :]
    rank_here = jnp.sum((same_source & earlier).astype(jnp.int32), axis=1)
    flat_index = sources * capacity + rank_here
    fetched = jnp.take(incoming.reshape(readers * capacity, PLEN, feat_width), flat_index, axis=0)
    passage_rows = fetched.reshape(per_reader * PLEN, feat_width)
    question_rows = questions.reshape(q_count * QLEN, feat_width)
    local_rows = jnp.concatenate([passage_rows, question_rows], axis=0)
    head_width = w_query.shape[1]
    full_rows, full_gain = (
        lax.all_gather(local_rows, "tp", axis=1, tiled=True),
        lax.all_gather(norm_gain, "tp", axis=1, tiled=True),
    )
    rows_wide = full_rows.astype(jnp.float32)
    factor = lax.rsqrt(jnp.mean(rows_wide * rows_wide, axis=1, keepdims=True) + 1e-06)
    normed = (rows_wide * factor * full_gain.astype(jnp.float32)).astype(jnp.bfloat16)
    queries = jnp.dot(normed, w_query, preferred_element_type=jnp.float32)
    keys_all = jnp.dot(normed, w_key, preferred_element_type=jnp.float32)
    values_all = jnp.dot(normed, w_value, preferred_element_type=jnp.float32)
    head_count = head_width // HDIM
    seq_total = QLEN + PLEN
    shape_heads = (q_count, NPASS, seq_total, head_count, HDIM)
    query_pairs = pair_layout(queries.astype(jnp.bfloat16), q_count, head_width).reshape(
        shape_heads
    )
    key_pairs = pair_layout(keys_all.astype(jnp.bfloat16), q_count, head_width).reshape(shape_heads)
    value_pairs = pair_layout(values_all.astype(jnp.bfloat16), q_count, head_width).reshape(
        shape_heads
    )
    scores = jnp.einsum(
        "bnqhe,bnkhe->bnhqk", query_pairs, key_pairs, preferred_element_type=jnp.float32
    )
    scores = scores - jnp.max(scores, axis=-1, keepdims=True)
    expd = jnp.exp(scores)
    probs = (expd / jnp.sum(expd, axis=-1, keepdims=True)).astype(jnp.bfloat16)
    context = jnp.einsum(
        "bnhqk,bnkhe->bnqhe", probs, value_pairs, preferred_element_type=jnp.float32
    )
    out_rows = q_count * NPASS * seq_total
    context = context.astype(jnp.bfloat16).reshape(out_rows, head_width)
    residual = pair_layout(local_rows, q_count, feat_width).reshape(out_rows, feat_width)
    partial_terms = jnp.dot(context, w_out, preferred_element_type=jnp.float32)
    branch = lax.psum_scatter(partial_terms, "tp", scatter_dimension=1, tiled=True)
    mixed = (residual.astype(jnp.float32) + branch).astype(jnp.bfloat16)
    return mixed.reshape(q_count, NPASS, seq_total, feat_width)


def solution(mesh):
    in_specs = (
        P(("groups", "mem"), None, "tp"),
        P(("groups", "mem"), None, "tp"),
        P("groups", None),
        P("groups"),
        P(None, "tp"),
        P(None, "tp"),
        P(None, "tp"),
        P(None, "tp"),
        P("tp", None),
    )
    out_specs = P(("groups", "mem"), None, None, "tp")
    return jax.shard_map(local, mesh=mesh, in_specs=in_specs, out_specs=out_specs, check_vma=False)
```

profile of v0, /device:TPU:0, one launch (start us, length us, event | category | flops | bytes accessed | tf_op | source)
XLA Modules:
  0.0 996.9 jit_solution(11705210762525744215)
XLA Ops:
  6.5 0.8 copy.25
  7.3 1.0 select_reduce_fusion
  8.5 0.4 convert_reduce_fusion
  9.0 0.3 select_reduce_fusion.1
  9.4 0.3 fusion.23
  9.9 8.0 gather_fusion
  17.9 5.4 select_select_fusion
  23.3 5.1 all-to-all-start
  28.5 0.5 broadcast.318
  29.0 1.1 fusion.41
  30.6 57.9 %all-to-all-done = bf16[4,10,64,1024]{3,2,1,0:T(8,128)(2,1)} async-done(((bf16[4,10,64,1024]{3,2,1,0:T(8,128)(2,1)}), bf16[4,10,64,1024]{3,2,1,0:T(8,128)(2,1)}, u32[]{:S(2)}, u32[]{:S(2)}) %all-to-all-start) | async-done | bytes 5242912 | tf_op jit(solution)/shard_map/all_to_all | solution.py:46
  88.5 3.2 gather_fusion.1
  91.8 0.5 bitcast_select_fusion
  92.2 1.9 pad_maximum_fusion.1
  94.2 14.2 %all_gather.7 = bf16[1,4096]{1,0:T(2,128)(2,1)S(1)} all-gather(bf16[1,1024]{1,0:T(2,128)(2,1)S(1)} %copy-done.9), channel_id=1, replica_groups=mesh['groups'=2,'mem'=4,'tp'=4] {'tp'}, dimensions={1}, use_global_device_ids=true | all-gather | bytes 10240 | tf_op jit(solution)/shard_map/all_gather | solution.py:58
  108.5 179.5 %all-gather.2.cloned.1.call-done = bf16[1344,4096]{1,0:T(8,128)(2,1)} async-done(((bf16[1344,1024]{1,0:T(8,128)(2,1)}), bf16[1344,4096]{1,0:T(8,128)(2,1)}) %all-gather.2.cloned.1.call-update) | async-done | bytes 11010064 | tf_op jit(solution)/shard_map/all_gather | solution.py:57
  288.0 6.5 fusion.1
  294.5 0.7 copy-done.2
  295.3 14.7 %convolution_convert_fusion = bf16[1344,1024]{1,0:T(8,128)(2,1)S(1)} fusion(bf16[4096,1024]{1,0:T(8,128)(2,1)} %param.15, bf16[1344,4096]{1,0:T(8,128)(2,1)S(1)} %copy-done.2, f32[4096]{0:T(1024)S(1)} %bitcast.53, f32[1344]{0:T(1024)S(1)} %add_rsqrt_fusion), kind=kOutput, calls=%fused_computation.26 | convolution fusion | flops 11297685504 | bytes 22172928 | tf_op jit(solution)/shard_map/dot_general | solution.py:64
  310.0 1.6 copy-done.5
  311.6 15.2 %convolution_convert_fusion.1 = bf16[1344,1024]{1,0:T(8,128)(2,1)S(1)} fusion(bf16[4096,1024]{1,0:T(8,128)(2,1)} %param.14, bf16[1344,4096]{1,0:T(8,128)(2,1)S(1)} %copy-done.2, f32[4096]{0:T(1024)S(1)} %bitcast.54, f32[1344]{0:T(1024)S(1)} %add_rsqrt_fusion), kind=kOutput, calls=%fused_computation.27 | convolution fusion | flops 11297685504 | bytes 22172928 | tf_op jit(solution)/shard_map/dot_general | solution.py:63
  326.9 1.5 copy-done.4
  328.4 12.4 %convolution_convert_fusion.2 = bf16[1344,1024]{1,0:T(8,128)(2,1)S(1)} fusion(bf16[4096,1024]{1,0:T(8,128)(2,1)S(1)} %bitcast.57, bf16[1344,4096]{1,0:T(8,128)(2,1)S(1)} %copy-done.2, f32[4096]{0:T(1024)S(1)} %bitcast.55, f32[1344]{0:T(1024)S(1)} %add_rsqrt_fusion), kind=kOutput, calls=%fused_computation.28 | convolution fusion | flops 11297685504 | bytes 22172928 | tf_op jit(solution)/shard_map/dot_general | solution.py:65
  340.8 1.5 copy-done.3
  342.3 1.2 slice-done.4
  343.5 4.9 concatenate.30
  348.4 8.3 copy.36
  356.9 0.3 copy.35
  357.2 5.0 concatenate.28
  362.2 8.3 copy.34
  370.7 1.1 copy.33
  371.7 4.9 concatenate.26
  376.6 8.3 copy.32
  385.1 0.3 copy.31
  385.4 3.6 broadcast_in_dim.126
  389.0 3.6 broadcast_in_dim.124
  392.6 17.0 %fusion.42 = (f32[2,10,16,96]{3,2,1,0:T(8,128)S(1)}, f32[2,10,16,96,96]{3,4,2,1,0:T(8,128)}) fusion(bf16[2,10,64,16,64]{2,4,3,1,0:T(8,128)(2,1)} %copy.34, bf16[2,10,32,16,64]{2,4,3,1,0:T(8,128)(2,1)} %broadcast_in_dim.124, bf16[2,10,64,16,64]{2,4,3,1,0:T(8,128)(2,1)} %copy.36, bf16[2,10,32,16,64]{2,4,3,1,0:T(8,128)(2,1)} %broadcast_in_dim.126), kind=kOutput, calls=%fused_computation.89 | convolution fusion | flops 399114336 | bytes 19783680 | tf_op jit(solution)/shard_map/sub | solution.py:79
  409.7 1.3 broadcast_in_dim.122
  411.0 10.5 %convert_bitcast_fusion = bf16[2,10,96,16,64]{2,4,3,1,0:T(8,128)(2,1)} fusion(f32[2,10,16,96,96]{3,4,2,1,0:T(8,128)} %get-tuple-element.8, f32[2,10,16,96]{3,2,1,0:T(8,128)S(1)} %get-tuple-element.7, bf16[2,10,64,16,64]{2,4,3,1,0:T(8,128)(2,1)} %copy.32, bf16[2,10,32,16,64]{2,4,3,1,0:T(8,128)(2,1)S(1)} %broadcast_in_dim.122), kind=kOutput, calls=%fused_computation.23 | convolution fusion | flops 393216000 | bytes 19783680 | tf_op jit(solution)/shard_map/bnhqk,bnkhe->bnqhe/dot_general | solution.py:82
  421.5 10.8 %copy.38 = bf16[2,10,96,16,64]{4,3,2,1,0:T(8,128)(2,1)} copy(bf16[2,10,96,16,64]{2,4,3,1,0:T(8,128)(2,1)} %convert_bitcast_fusion) | data formatting | bytes 7864320 | tf_op jit(solution)/shard_map/convert_element_type | solution.py:86
  432.2 11.4 %reshape.278 = bf16[1920,1024]{1,0:T(8,128)(2,1)} reshape(bf16[2,10,96,16,64]{4,3,2,1,0:T(8,128)(2,1)} %copy.38) | data formatting | bytes 7864320 | tf_op jit(solution)/shard_map/reshape | solution.py:86
  443.6 24.7 %fusion.47 = f32[1920,4096]{1,0:T(8,128)} fusion(bf16[1920,1024]{1,0:T(8,128)(2,1)} %reshape.278, bf16[1024,4096]{1,0:T(8,128)(2,1)} %param.17), kind=kOutput, calls=%fused_computation.90 | convolution fusion | flops 16106127360 | bytes 43778048 | tf_op jit(solution)/shard_map/dot_general | solution.py:88
  468.3 0.6 copy-done.12
  469.1 0.9 copy-done.1
  470.0 0.3 broadcast_select_fusion
  470.5 2.4 pad_maximum_fusion
  472.9 509.2 %reduce-scatter.2.cloned.1.call-done = f32[1920,1024]{1,0:T(8,128)} async-done(((f32[1920,4096]{1,0:T(8,128)}), f32[1920,1024]{1,0:T(8,128)}) %reduce-scatter.2.cloned.1.call-update) | async-done | bytes 7864336 | tf_op jit(solution)/shard_map/reduce_scatter | solution.py:89
  982.1 7.8 fusion.4
  (70 shorter events, 2.2 us)
Async XLA Ops:
  23.3 65.1 %all-to-all-start = ((bf16[4,10,64,1024]{3,2,1,0:T(8,128)(2,1)}), bf16[4,10,64,1024]{3,2,1,0:T(8,128)(2,1)}, u32[]{:S(2)}, u32[]{:S(2)}) async-start(bf16[4,10,64,1024]{3,2,1,0:T(8,128)(2,1)} %select_select_fusion), calls=%async_computation | async-start | bytes 10485760 | tf_op jit(solution)/shard_map/all_to_all | solution.py:46
  28.4 259.5 %all-gather.2.cloned.1.call-start = ((), (), s32[]{:S(2)}) async-start(), calls=%async_computation.2 | async-start | bytes 13762560 | tf_op jit(solution)/shard_map/all_gather | solution.py:57
  30.4 58.1 %copy-start.11 = (s32[20]{0:T(128)}, s32[20]{0:T(128)S(1)}, u32[]{:S(2)}) copy-start(s32[20]{0:T(128)S(1)} %convert_reduce_fusion.1) | copy-start | bytes 244
  88.5 3.7 copy-start.7
  91.7 2.4 copy-start
  92.2 2.0 copy-start.9
  94.2 887.9 %reduce-scatter.2.cloned.1.call-start = ((), (), s32[]{:S(2)}) async-start(), calls=%async_computation.3 | async-start | bytes 39321600 | tf_op jit(solution)/shard_map/reduce_scatter | solution.py:89
  288.0 7.3 copy-start.2
  310.0 1.6 copy-start.5
  310.0 18.4 %slice-start.6 = ((s8[8388608]{0:T(1024)(128)(4,1)}), s8[4194304]{0:T(1024)(128)(4,1)S(1)}, s32[]{:S(2)}) async-start(s8[8388608]{0:T(1024)(128)(4,1)} %bitcast.56), calls=%async_computation.10 | async-start | bytes 8388608
  311.6 16.8 %slice-start.7 = ((s8[8388608]{0:T(1024)(128)(4,1)}), s8[4194304]{0:T(1024)(128)(4,1)S(1)}, s32[]{:S(2)}) async-start(s8[8388608]{0:T(1024)(128)(4,1)} %bitcast.56), calls=%async_computation.11 | async-start | bytes 8388608
  326.9 1.5 copy-start.4
  340.8 1.5 copy-start.3
  340.8 2.7 slice-start.4
  348.4 8.3 slice-start.5
  348.4 8.8 slice-start.2
  362.2 8.3 slice-start.3
  362.2 9.5 slice-start
  376.6 8.3 slice-start.1
  384.9 4.1 copy-start.6
  468.3 0.7 copy-start.12
  468.3 0.8 copy-start.10
  468.3 1.7 copy-start.1
  469.0 1.4 copy-start.8
Sparse Core Ops, SparseCore 0:
  94.3 193.6 all-gather.1
  468.4 513.6 reduce-scatter.1
where the time goes:
time: 1000 us; the launch traced here: 997 us
  waiting for transfers between devices  747 us (75%)
  local copies, waits for them, and re-layouts  95.5 us (10%)
  matrix products  94.5 us (9%)
  other arithmetic  27 us (3%)
  blocking collectives  14.2 us (1%)
  between operations  13.9 us (1%)
    reduce_scatter x1, waiting for transfers between devices, local(): lax.psum_scatter(partial_terms, 'tp', scatter_dimension=1, tiled=True)  509 us
    all_gather x1, waiting for transfers between devices, local(): lax.all_gather(local_rows, 'tp', axis=1, tiled=True)  180 us
    all_to_all x1, waiting for transfers between devices, local(): lax.all_to_all(outgoing, 'mem', split_axis=0, concat_axis=0, tiled=True)  57.9 us
    concatenate x6, local copies, waits for them, and re-layouts, pair_layout(): return jnp.concatenate([ques_part, pass_part], axis=2)  39.6 us
    dot_general x1, matrix products, local(): partial_terms = jnp.dot(context, w_out, preferred_element_type=jnp.float32)  24.7 us
  transfers between devices with their start and end apart: 3, of which 3 were waited for; matrix products, arithmetic and copies ran while one was open for 1% of the time, Pallas kernels for 0%

commit v1 on v0

v1 whole, which is shorter than its diff:
```python
import jax
import jax.numpy as jnp
from jax import lax
from jax.experimental import pallas as pl
from jax.experimental.pallas import tpu as pltpu
from jax.sharding import PartitionSpec as P

HDIM = 64
PLEN = 64
GATHER = "native"
REDUCE = "native"
CHUNKS = 5
RING_MAX = 8


def line_gather(rows, axis):
    n = lax.axis_size(axis)
    if GATHER == "native" or n > RING_MAX:
        return lax.all_gather(rows, axis, axis=1, tiled=True)
    width = rows.shape[1]
    from_left, from_right = [], []
    right, left = rows, rows
    for step in range(1, n):
        right = lax.ppermute(right, axis, [(i, i + 1) for i in range(step - 1, n - 1)])
        left = lax.ppermute(left, axis, [(i, i - 1) for i in range(1, n - step + 1)])
        from_left.append(right)
        from_right.append(left)
    strip = jnp.concatenate(from_left[::-1] + [rows] + from_right, axis=1)
    me = lax.axis_index(axis)
    return lax.dynamic_slice_in_dim(strip, (n - 1 - me) * width, n * width, 1)


def line_reduce(terms, axis):
    n = lax.axis_size(axis)
    if REDUCE == "native" or n > RING_MAX:
        return lax.psum_scatter(terms, axis, scatter_dimension=1, tiled=True).astype(jnp.float32)
    width = terms.shape[1] // n
    me = lax.axis_index(axis)

    def block(index):
        start = jnp.clip(index, 0, n - 1) * width
        return lax.dynamic_slice_in_dim(terms, start, width, 1)

    right = left = None
    for step in range(1, n):
        reach = n - step
        out_right, out_left = block(me + reach), block(me - reach)
        if step > 1:
            out_right = (out_right.astype(jnp.float32) + right.astype(jnp.float32)).astype(jnp.bfloat16)
            out_left = (out_left.astype(jnp.float32) + left.astype(jnp.float32)).astype(jnp.bfloat16)
        right = lax.ppermute(out_right, axis, [(i, i + 1) for i in range(step)])
        left = lax.ppermute(out_left, axis, [(i, i - 1) for i in range(n - step, n)])
    return block(me).astype(jnp.float32) + right.astype(jnp.float32) + left.astype(jnp.float32)


def attend_kernel(ques_ref, qq, kq, vq, qp, kp, vp, out):
    del ques_ref
    total = qq.shape[0] + qp.shape[0]
    first = lax.broadcasted_iota(jnp.int32, (total, 2 * HDIM), 1) < HDIM
    zero = jnp.zeros((total, 2 * HDIM), jnp.bfloat16)
    for j in range(qq.shape[1] // (2 * HDIM)):
        cols = slice(j * 2 * HDIM, (j + 1) * 2 * HDIM)
        q = jnp.concatenate([qq[:, cols], qp[:, cols]], axis=0)
        k = jnp.concatenate([kq[:, cols], kp[:, cols]], axis=0)
        v = jnp.concatenate([vq[:, cols], vp[:, cols]], axis=0)
        both = jnp.concatenate([jnp.where(first, q, zero), jnp.where(first, zero, q)], axis=0)
        scores = lax.dot_general(both, k, (((1,), (1,)), ((), ())), preferred_element_type=jnp.float32)
        expd = jnp.exp(scores - jnp.max(scores, axis=-1, keepdims=True))
        probs = (expd / jnp.sum(expd, axis=-1, keepdims=True)).astype(jnp.bfloat16)
        ctx = jnp.dot(probs, v, preferred_element_type=jnp.float32)
        out[:, cols] = jnp.where(first, ctx[:total], ctx[total:]).astype(jnp.bfloat16)


def attend(question_of, ques, passages, qlen):
    count = question_of.shape[0]
    width = ques[0].shape[1]
    seq = qlen + PLEN
    ques_spec = pl.BlockSpec((qlen, width), lambda i, q: (q[i], 0))
    pass_spec = pl.BlockSpec((PLEN, width), lambda i, q: (i, 0))
    return pl.pallas_call(
        attend_kernel,
        grid_spec=pltpu.PrefetchScalarGridSpec(
            num_scalar_prefetch=1,
            grid=(count,),
            in_specs=[ques_spec] * 3 + [pass_spec] * 3,
            out_specs=pl.BlockSpec((seq, width), lambda i, q: (i, 0)),
        ),
        out_shape=jax.ShapeDtypeStruct((count * seq, width), jnp.bfloat16),
        cost_estimate=pl.CostEstimate(
            flops=8 * count * seq * seq * width,
            bytes_accessed=8 * count * seq * width,
            transcendentals=count * seq * seq * width // HDIM,
        ),
    )(question_of, *ques, *passages)


def normalize(rows, gain):
    wide = rows.astype(jnp.float32)
    factor = lax.rsqrt(jnp.mean(wide * wide, axis=1, keepdims=True) + 1e-06)
    return (wide * factor * gain.astype(jnp.float32)).astype(jnp.bfloat16)


def project(rows, weights):
    return [jnp.dot(rows, w, preferred_element_type=jnp.float32).astype(jnp.bfloat16) for w in weights]


def local(questions, memory, pass_ids, pass_map, norm_gain, w_query, w_key, w_value, w_out):
    readers = lax.axis_size("mem")
    own_index = lax.axis_index("mem")
    q_count, qlen, feat_width = questions.shape
    npass = pass_ids.shape[1]
    slot_count = memory.shape[0]
    stored = pass_map.shape[0]
    per_reader = q_count * npass
    capacity = min(per_reader, 2 * -(-per_reader // readers))
    weights = (w_query, w_key, w_value)

    matches = pass_ids[:, :, None] == jnp.arange(stored, dtype=jnp.int32)[None, None, :]
    location = jnp.sum(jnp.where(matches, pass_map[None, None, :], 0), axis=2).reshape(readers, per_reader)
    owners = location // slot_count
    position = jnp.arange(per_reader, dtype=jnp.int32)
    earlier = position[:, None] > position[None, :]
    mine = owners == own_index
    rank_mine = jnp.sum((mine[:, None, :] & earlier[None, :, :]).astype(jnp.int32), axis=2)
    slot_ids = jnp.arange(capacity, dtype=jnp.int32)
    pick = mine[:, None, :] & (rank_mine[:, None, :] == slot_ids[None, :, None])
    slot_rows = jnp.sum(jnp.where(pick, (location % slot_count)[:, None, :], 0), axis=2)

    sources = lax.dynamic_index_in_dim(owners, own_index, 0, keepdims=False)
    same_source = sources[:, None] == sources[None, :]
    rank_here = jnp.sum((same_source & earlier).astype(jnp.int32), axis=1)
    order_key = rank_here * per_reader + position
    place = jnp.sum((order_key[None, :] < order_key[:, None]).astype(jnp.int32), axis=1)
    at_place = place[None, :] == position[:, None]

    def in_order(values):
        return jnp.sum(jnp.where(at_place, values[None, :], 0), axis=1)

    listed = in_order(position)
    source_of, rank_of = in_order(sources), in_order(rank_here)
    question_of = listed // npass

    chunks = CHUNKS if per_reader % CHUNKS == 0 and capacity % CHUNKS == 0 else 1
    ranks, count = capacity // chunks, per_reader // chunks
    slot_of = ((rank_of // ranks) * readers + source_of) * ranks + rank_of % ranks

    question_rows = questions.reshape(q_count * qlen, feat_width)
    head_rows = line_gather(jnp.concatenate([question_rows, norm_gain], axis=0), "tp")
    gain = head_rows[q_count * qlen :]
    ques_qkv = project(normalize(head_rows[: q_count * qlen], gain), weights)

    incoming, finished = [], []
    for c in range(chunks):
        rows = slot_rows[:, c * ranks : (c + 1) * ranks]
        picked = jnp.take(memory, rows.reshape(-1), axis=0).reshape(readers, ranks, PLEN, feat_width)
        arrived = lax.all_to_all(picked, "mem", split_axis=0, concat_axis=0, tiled=True)
        incoming.append(arrived.reshape(readers * ranks, PLEN, feat_width))
        part = slice(c * count, (c + 1) * count)
        pool = jnp.concatenate(incoming, axis=0) if c else incoming[0]
        fetched = jnp.take(pool, slot_of[part], axis=0)
        full = line_gather(fetched.reshape(count * PLEN, feat_width), "tp")
        pass_qkv = project(normalize(full, gain), weights)
        context = attend(question_of[part], ques_qkv, pass_qkv, qlen)
        terms = jnp.dot(context, w_out, preferred_element_type=jnp.float32).astype(jnp.bfloat16)
        branch = line_reduce(terms, "tp").reshape(count, qlen + PLEN, feat_width)
        residual = jnp.concatenate([jnp.take(questions, question_of[part], axis=0), fetched], axis=1)
        finished.append((residual.astype(jnp.float32) + branch).astype(jnp.bfloat16))
    mixed = jnp.take(jnp.concatenate(finished, axis=0), place, axis=0)
    return mixed.reshape(q_count, npass, qlen + PLEN, feat_width)


def solution(mesh):
    in_specs = (
        P(("groups", "mem"), None, "tp"),
        P(("groups", "mem"), None, "tp"),
        P("groups", None),
        P("groups"),
        P(None, "tp"),
        P(None, "tp"),
        P(None, "tp"),
        P(None, "tp"),
        P("tp", None),
    )
    out_specs = P(("groups", "mem"), None, None, "tp")
    return jax.shard_map(local, mesh=mesh, in_specs=in_specs, out_specs=out_specs, check_vma=False)
```

time: 1000 us -> 616 us (0.62)
  waiting for transfers between devices: 747 us -> 246 us
  matrix products: 94.5 us -> 141 us
  other arithmetic: 27 us -> 66.9 us
  local copies, waits for them, and re-layouts: 95.5 us -> 57.1 us
  Pallas kernels: 0 us -> 34.1 us
  starting transfers between devices: 5.17 us -> 22.1 us
  blocking collectives: 14.2 us -> 25 us
    reduce_scatter x1 -> x5, waiting for transfers between devices: 509 us -> 204 us  [line_reduce(): lax.psum_scatter(terms, axis, scatter_dimension=1, tiled=True)]
    all_gather x1 -> x5, waiting for transfers between devices: 180 us -> 0.09 us  [line_gather(): return lax.all_gather(rows, axis, axis=1, tiled=True)]
    dot_general x5 -> x23, matrix products: 77.5 us -> 141 us  [the longest x18 97 us: project(): jnp.dot(rows, w, preferred_element_type=jnp.float32).astype(jnp.bfloat16)]
    concatenate x6 -> x1, local copies, waits for them, and re-layouts: 39.6 us -> 2.29 us  [local(): pool = jnp.concatenate(incoming, axis=0) if c else incoming[0]]
    pallas_call x0 -> x5, Pallas kernels: none -> 34.1 us  [attend(): pl.pallas_call(attend_kernel, grid_spec=pltpu.PrefetchScalarGridSpec(num_...]
    gather x2 -> x16, local copies, waits for them, and re-layouts: 11.2 us -> 43.4 us  [the longest x5 23.1 us: local(): jnp.take(memory, rows.reshape(-1), axis=0)]
    select_n x6 -> x28, other arithmetic: 6.23 us -> 29.9 us  [the longest x10 9.4 us: local(): jnp.take(memory, rows.reshape(-1), axis=0)]
    sub x1 -> x0, matrix products: 17 us -> none  [local(): scores = scores - jnp.max(scores, axis=-1, keepdims=True)]
  transfers between devices with their start and end apart: 3 -> 15, of which waited for: 3 -> 7; matrix products, arithmetic and copies ran while one was open for 1% -> 40% of each run, Pallas kernels for 0% -> 6%
where the time goes in v1:
time: 616 us; the launch traced here: 606 us
  waiting for transfers between devices  246 us (40%)
  matrix products  141 us (23%)
  other arithmetic  66.9 us (11%)
  local copies, waits for them, and re-layouts  57.1 us (9%)
  Pallas kernels  34.1 us (6%)
  blocking collectives  25 us (4%)
  starting transfers between devices  22.1 us (4%)
  between operations  14.8 us (2%)
    reduce_scatter x5, waiting for transfers between devices, line_reduce(): lax.psum_scatter(terms, axis, scatter_dimension=1, tiled=True)  204 us
    dot_general x18, matrix products, project(): jnp.dot(rows, w, preferred_element_type=jnp.float32).astype(jnp.bfloat16)  97 us
    dot_general x5, matrix products, local(): jnp.dot(context, w_out, preferred_element_type=jnp.float32)  43.8 us
    all_to_all x5, waiting for transfers between devices, local(): lax.all_to_all(picked, 'mem', split_axis=0, concat_axis=0, tiled=True)  41.3 us
    pallas_call x5, Pallas kernels, attend(): pl.pallas_call(attend_kernel, grid_spec=pltpu.PrefetchScalarGridSpec(num_...  34.1 us
    all_gather x1, blocking collectives, line_gather(): return lax.all_gather(rows, axis, axis=1, tiled=True)  25 us
    gather x5, local copies, waits for them, and re-layouts, local(): jnp.take(memory, rows.reshape(-1), axis=0)  23.1 us
    all_to_all x5, starting transfers between devices, local(): lax.all_to_all(picked, 'mem', split_axis=0, concat_axis=0, tiled=True)  20.5 us
  transfers between devices with their start and end apart: 15, of which 7 were waited for; matrix products, arithmetic and copies ran while one was open for 40% of the time, Pallas kernels for 6%

profile of v1, /device:TPU:0, one launch (start us, length us, event | category | flops | bytes accessed | tf_op | source)
XLA Modules:
  0.0 606.3 jit_solution(7222890163740952197)
XLA Ops:
  9.5 4.0 gather_fusion.7
  14.6 4.2 all-to-all-start
  20.1 13.2 %all-to-all-done = bf16[4,2,64,1024]{3,2,1,0:T(8,128)(2,1)S(1)} async-done(((bf16[4,2,64,1024]{3,2,1,0:T(8,128)(2,1)}), bf16[4,2,64,1024]{3,2,1,0:T(8,128)(2,1)S(1)}, u32[]{:S(2)}, u32[]{:S(2)}) %all-to-all-start) | async-done | bytes 1048608 | tf_op jit(solution)/shard_map/all_to_all | solution.py:156
  35.3 4.0 gather_fusion.9
  40.5 3.5 all-to-all-start.1
  44.2 14.2 %all-to-all-done.1 = bf16[4,2,64,1024]{3,2,1,0:T(8,128)(2,1)S(1)} async-done(((bf16[4,2,64,1024]{3,2,1,0:T(8,128)(2,1)}), bf16[4,2,64,1024]{3,2,1,0:T(8,128)(2,1)S(1)}, u32[]{:S(2)}, u32[]{:S(2)}) %all-to-all-start.1) | async-done | bytes 1048608 | tf_op jit(solution)/shard_map/all_to_all | solution.py:156
  63.2 5.0 gather_fusion.11
  70.5 4.2 all-to-all-start.2
  75.4 13.9 %all-to-all-done.2 = bf16[4,2,64,1024]{3,2,1,0:T(8,128)(2,1)} async-done(((bf16[4,2,64,1024]{3,2,1,0:T(8,128)(2,1)}), bf16[4,2,64,1024]{3,2,1,0:T(8,128)(2,1)}, u32[]{:S(2)}, u32[]{:S(2)}) %all-to-all-start.2) | async-done | bytes 1048608 | tf_op jit(solution)/shard_map/all_to_all | solution.py:156
  95.7 5.0 gather_fusion.13
  103.2 4.3 all-to-all-start.3
  107.4 5.0 gather_fusion.15
  112.7 25.0 %all_gather.18 = bf16[65,4096]{1,0:T(8,128)(2,1)S(1)} all-gather(bf16[65,1024]{1,0:T(8,128)(2,1)S(1)} %pad_maximum_fusion.3), channel_id=1, replica_groups=mesh['groups'=2,'mem'=4,'tp'=4] {'tp'}, dimensions={1}, use_global_device_ids=true | all-gather | bytes 665600 | tf_op jit(solution)/shard_map/all_gather | solution.py:19
  140.3 4.2 all-to-all-start.4
  144.6 4.2 pad_maximum_fusion
  152.6 5.8 convolution_convert_fusion.20.vq
  158.5 5.8 convolution_convert_fusion.21.kq
  183.2 7.3 %convolution_convert_fusion.17.vp = bf16[256,1024]{1,0:T(8,128)(2,1)} fusion(bf16[4096,1024]{1,0:T(8,128)(2,1)} %param.20, bf16[256,4096]{1,0:T(8,128)(2,1)} %all-gather.6.cloned.1.call-done, f32[4096]{0:T(1024)S(1)} %bitcast.99, f32[256]{0:T(256)S(1)} %add_rsqrt_fusion.4), kind=kOutput, calls=%fused_computation.74 | convolution fusion | flops 2151940096 | bytes 11027456 | tf_op jit(solution)/shard_map/dot_general | solution.py:104
  190.6 3.2 convolution_convert_fusion.18.kp
  193.8 3.2 convolution_convert_fusion.19.qp
  196.9 6.8 %shard_map.91 = bf16[384,1024]{1,0:T(8,128)(2,1)} custom-call(s32[4]{0:T(128)} %get-tuple-element.57.ques_ref, bf16[64,1024]{1,0:T(8,128)(2,1)} %convolution_convert_fusion.22.qq, bf16[64,1024]{1,0:T(8,128)(2,1)} %convolution_convert_fusion.21.kq, bf16[64,1024]{1,0:T(8,128)(2,1)} %convolution_convert_fusion.20.vq, ...), custom_call_target="tpu_custom_call" | custom-call | flops 301989888 | bytes 3145728 | tf_op jit(solution)/shard_map/pallas_call | solution.py:80
  203.7 8.8 %convolution_convert_fusion.4 = bf16[384,4096]{1,0:T(8,128)(2,1)} fusion(bf16[384,1024]{1,0:T(8,128)(2,1)} %shard_map.91, bf16[1024,4096]{1,0:T(8,128)(2,1)} %param.21), kind=kOutput, calls=%fused_computation.20 | convolution fusion | flops 3222798336 | bytes 12320768 | tf_op jit(solution)/shard_map/dot_general | solution.py:164
  215.1 7.4 %convolution_convert_fusion.14.vp = bf16[256,1024]{1,0:T(8,128)(2,1)} fusion(bf16[4096,1024]{1,0:T(8,128)(2,1)} %param.20, bf16[256,4096]{1,0:T(8,128)(2,1)} %all-gather.8.cloned.1.call-done, f32[256]{0:T(256)S(1)} %add_rsqrt_fusion.3, f32[4096]{0:T(1024)S(1)} %bitcast.102), kind=kOutput, calls=%fused_computation.71 | convolution fusion | flops 2151940096 | bytes 11027456 | tf_op jit(solution)/shard_map/dot_general | solution.py:104
  222.5 6.7 %convolution_convert_fusion.15.kp = bf16[256,1024]{1,0:T(8,128)(2,1)} fusion(bf16[4096,1024]{1,0:T(8,128)(2,1)} %param.19, bf16[256,4096]{1,0:T(8,128)(2,1)S(1)} %copy-done.13, f32[256]{0:T(256)S(1)} %add_rsqrt_fusion.3, f32[4096]{0:T(1024)S(1)} %bitcast.103), kind=kOutput, calls=%fused_computation.72 | convolution fusion | flops 2151940096 | bytes 11027456 | tf_op jit(solution)/shard_map/dot_general | solution.py:104
  229.2 3.2 convolution_convert_fusion.16.qp
  232.4 6.8 %shard_map.92 = bf16[384,1024]{1,0:T(8,128)(2,1)} custom-call(s32[4]{0:T(128)} %get-tuple-element.56.ques_ref, bf16[64,1024]{1,0:T(8,128)(2,1)} %convolution_convert_fusion.22.qq, bf16[64,1024]{1,0:T(8,128)(2,1)} %convolution_convert_fusion.21.kq, bf16[64,1024]{1,0:T(8,128)(2,1)} %convolution_convert_fusion.20.vq, ...), custom_call_target="tpu_custom_call" | custom-call | flops 301989888 | bytes 3145728 | tf_op jit(solution)/shard_map/pallas_call | solution.py:80
  239.2 8.7 %convolution_convert_fusion.3 = bf16[384,4096]{1,0:T(8,128)(2,1)} fusion(bf16[384,1024]{1,0:T(8,128)(2,1)} %shard_map.92, bf16[1024,4096]{1,0:T(8,128)(2,1)} %param.21), kind=kOutput, calls=%fused_computation.19 | convolution fusion | flops 3222798336 | bytes 12320768 | tf_op jit(solution)/shard_map/dot_general | solution.py:164
  250.3 7.4 %convolution_convert_fusion.11.vp = bf16[256,1024]{1,0:T(8,128)(2,1)} fusion(bf16[4096,1024]{1,0:T(8,128)(2,1)} %param.20, bf16[256,4096]{1,0:T(8,128)(2,1)} %all-gather.10.cloned.1.call-done, f32[256]{0:T(256)S(1)} %add_rsqrt_fusion.2, f32[4096]{0:T(1024)S(1)} %bitcast.105), kind=kOutput, calls=%fused_computation.68 | convolution fusion | flops 2151940096 | bytes 11027456 | tf_op jit(solution)/shard_map/dot_general | solution.py:104
  257.7 6.8 %convolution_convert_fusion.12.kp = bf16[256,1024]{1,0:T(8,128)(2,1)} fusion(bf16[4096,1024]{1,0:T(8,128)(2,1)} %param.19, bf16[256,4096]{1,0:T(8,128)(2,1)S(1)} %copy-done.14, f32[256]{0:T(256)S(1)} %add_rsqrt_fusion.2, f32[4096]{0:T(1024)S(1)} %bitcast.106), kind=kOutput, calls=%fused_computation.69 | convolution fusion | flops 2151940096 | bytes 11027456 | tf_op jit(solution)/shard_map/dot_general | solution.py:104
  264.5 3.2 convolution_convert_fusion.13.qp
  267.7 6.8 %shard_map.93 = bf16[384,1024]{1,0:T(8,128)(2,1)} custom-call(s32[4]{0:T(128)} %get-tuple-element.55.ques_ref, bf16[64,1024]{1,0:T(8,128)(2,1)} %convolution_convert_fusion.22.qq, bf16[64,1024]{1,0:T(8,128)(2,1)} %convolution_convert_fusion.21.kq, bf16[64,1024]{1,0:T(8,128)(2,1)} %convolution_convert_fusion.20.vq, ...), custom_call_target="tpu_custom_call" | custom-call | flops 301989888 | bytes 3145728 | tf_op jit(solution)/shard_map/pallas_call | solution.py:80
  274.4 8.7 %convolution_convert_fusion.2 = bf16[384,4096]{1,0:T(8,128)(2,1)} fusion(bf16[384,1024]{1,0:T(8,128)(2,1)} %shard_map.93, bf16[1024,4096]{1,0:T(8,128)(2,1)} %param.21), kind=kOutput, calls=%fused_computation.18 | convolution fusion | flops 3222798336 | bytes 12320768 | tf_op jit(solution)/shard_map/dot_general | solution.py:164
  285.6 7.4 %convolution_convert_fusion.10.qp = bf16[256,1024]{1,0:T(8,128)(2,1)} fusion(bf16[4096,1024]{1,0:T(8,128)(2,1)} %param.18, bf16[256,4096]{1,0:T(8,128)(2,1)} %all-gather.12.cloned.1.call-done, f32[256]{0:T(256)S(1)} %add_rsqrt_fusion.1, f32[4096]{0:T(1024)S(1)} %bitcast.108), kind=kOutput, calls=%fused_computation.67 | convolution fusion | flops 2151940096 | bytes 11027456 | tf_op jit(solution)/shard_map/dot_general | solution.py:104
  292.9 6.8 %convolution_convert_fusion.8.vp = bf16[256,1024]{1,0:T(8,128)(2,1)} fusion(bf16[4096,1024]{1,0:T(8,128)(2,1)} %param.20, bf16[256,4096]{1,0:T(8,128)(2,1)S(1)} %copy-done.15, f32[256]{0:T(256)S(1)} %add_rsqrt_fusion.1, f32[4096]{0:T(1024)S(1)} %bitcast.109), kind=kOutput, calls=%fused_computation.65 | convolution fusion | flops 2151940096 | bytes 11027456 | tf_op jit(solution)/shard_map/dot_general | solution.py:104
  299.7 3.2 convolution_convert_fusion.9.kp
  302.9 6.8 %shard_map.94 = bf16[384,1024]{1,0:T(8,128)(2,1)} custom-call(s32[4]{0:T(128)} %get-tuple-element.54.ques_ref, bf16[64,1024]{1,0:T(8,128)(2,1)} %convolution_convert_fusion.22.qq, bf16[64,1024]{1,0:T(8,128)(2,1)} %convolution_convert_fusion.21.kq, bf16[64,1024]{1,0:T(8,128)(2,1)} %convolution_convert_fusion.20.vq, ...), custom_call_target="tpu_custom_call" | custom-call | flops 301989888 | bytes 3145728 | tf_op jit(solution)/shard_map/pallas_call | solution.py:80
  309.7 8.8 %convolution_convert_fusion.1 = bf16[384,4096]{1,0:T(8,128)(2,1)} fusion(bf16[384,1024]{1,0:T(8,128)(2,1)} %shard_map.94, bf16[1024,4096]{1,0:T(8,128)(2,1)} %param.21), kind=kOutput, calls=%fused_computation.17 | convolution fusion | flops 3222798336 | bytes 12320768 | tf_op jit(solution)/shard_map/dot_general | solution.py:164
  320.9 7.4 %convolution_convert_fusion.5.vp = bf16[256,1024]{1,0:T(8,128)(2,1)} fusion(bf16[4096,1024]{1,0:T(8,128)(2,1)} %param.20, bf16[256,4096]{1,0:T(8,128)(2,1)} %all-gather.14.cloned.1.call-done, f32[256]{0:T(256)S(1)} %add_rsqrt_fusion, f32[4096]{0:T(1024)S(1)} %bitcast.111), kind=kOutput, calls=%fused_computation.62 | convolution fusion | flops 2151940096 | bytes 11027456 | tf_op jit(solution)/shard_map/dot_general | solution.py:104
  328.4 6.7 %convolution_convert_fusion.6.kp = bf16[256,1024]{1,0:T(8,128)(2,1)} fusion(bf16[4096,1024]{1,0:T(8,128)(2,1)} %param.19, bf16[256,4096]{1,0:T(8,128)(2,1)S(1)} %copy-done.16, f32[256]{0:T(256)S(1)} %add_rsqrt_fusion, f32[4096]{0:T(1024)S(1)} %bitcast.112), kind=kOutput, calls=%fused_computation.63 | convolution fusion | flops 2151940096 | bytes 11027456 | tf_op jit(solution)/shard_map/dot_general | solution.py:104
  335.1 3.2 convolution_convert_fusion.7.qp
  338.2 7.0 %shard_map.95 = bf16[384,1024]{1,0:T(8,128)(2,1)} custom-call(s32[4]{0:T(128)} %get-tuple-element.53.ques_ref, bf16[64,1024]{1,0:T(8,128)(2,1)} %convolution_convert_fusion.22.qq, bf16[64,1024]{1,0:T(8,128)(2,1)} %convolution_convert_fusion.21.kq, bf16[64,1024]{1,0:T(8,128)(2,1)} %convolution_convert_fusion.20.vq, ...), custom_call_target="tpu_custom_call" | custom-call | flops 301989888 | bytes 3145728 | tf_op jit(solution)/shard_map/pallas_call | solution.py:80
  345.3 8.9 %convolution_convert_fusion = bf16[384,4096]{1,0:T(8,128)(2,1)} fusion(bf16[384,1024]{1,0:T(8,128)(2,1)} %shard_map.95, bf16[1024,4096]{1,0:T(8,128)(2,1)} %param.21), kind=kOutput, calls=%fused_computation.16 | convolution fusion | flops 3222798336 | bytes 12320768 | tf_op jit(solution)/shard_map/dot_general | solution.py:164
  376.1 23.3 %reduce-scatter.8.cloned.1.call-done = bf16[384,1024]{1,0:T(8,128)(2,1)} async-done(((bf16[384,4096]{1,0:T(8,128)(2,1)}), bf16[384,1024]{1,0:T(8,128)(2,1)}) %reduce-scatter.8.cloned.1.call-update) | async-done | bytes 786448 | tf_op jit(solution)/shard_map/reduce_scatter | solution.py:36
  401.8 60.2 %reduce-scatter.10.cloned.1.call-done = bf16[384,1024]{1,0:T(8,128)(2,1)} async-done(((bf16[384,4096]{1,0:T(8,128)(2,1)}), bf16[384,1024]{1,0:T(8,128)(2,1)}) %reduce-scatter.10.cloned.1.call-update) | async-done | bytes 786448 | tf_op jit(solution)/shard_map/reduce_scatter | solution.py:36
  464.4 60.3 %reduce-scatter.12.cloned.1.call-done = bf16[384,1024]{1,0:T(8,128)(2,1)} async-done(((bf16[384,4096]{1,0:T(8,128)(2,1)}), bf16[384,1024]{1,0:T(8,128)(2,1)}) %reduce-scatter.12.cloned.1.call-update) | async-done | bytes 786448 | tf_op jit(solution)/shard_map/reduce_scatter | solution.py:36
  527.0 60.1 %reduce-scatter.14.cloned.1.call-done = bf16[384,1024]{1,0:T(8,128)(2,1)} async-done(((bf16[384,4096]{1,0:T(8,128)(2,1)}), bf16[384,1024]{1,0:T(8,128)(2,1)}) %reduce-scatter.14.cloned.1.call-update) | async-done | bytes 786448 | tf_op jit(solution)/shard_map/reduce_scatter | solution.py:36
  589.5 5.0 gather_fusion.5
  594.5 4.5 broadcast_select_fusion
  (253 shorter events, 91.4 us)
Async XLA Ops:
  14.6 18.7 %all-to-all-start = ((bf16[4,2,64,1024]{3,2,1,0:T(8,128)(2,1)}), bf16[4,2,64,1024]{3,2,1,0:T(8,128)(2,1)S(1)}, u32[]{:S(2)}, u32[]{:S(2)}) async-start(bf16[4,2,64,1024]{3,2,1,0:T(8,128)(2,1)} %bitcast.1), calls=%async_computation | async-start | bytes 2097152 | tf_op jit(solution)/shard_map/all_to_all | solution.py:156
  18.8 162.1 %all-gather.6.cloned.1.call-start = ((), (), s32[]{:S(2)}) async-start(), calls=%async_computation.10 | async-start | bytes 2621440 | tf_op jit(solution)/shard_map/all_gather | solution.py:19
  19.8 147.1 %copy-start.19 = (s32[20]{0:T(128)}, s32[20]{0:T(128)S(1)}, u32[]{:S(2)}) copy-start(s32[20]{0:T(128)S(1)} %get-tuple-element.58) | copy-start | bytes 244
  19.9 20.6 %copy-start.29 = (pred[4]{0:T(512)(128)(4,1)}, pred[4]{0:T(512)(128)(4,1)S(1)}, u32[]{:S(2)}) copy-start(pred[4]{0:T(512)(128)(4,1)S(1)} %get-tuple-element.51) | copy-start | bytes 16
  19.9 24.2 %copy-start.28 = (pred[4]{0:T(512)(128)(4,1)}, pred[4]{0:T(512)(128)(4,1)S(1)}, u32[]{:S(2)}) copy-start(pred[4]{0:T(512)(128)(4,1)S(1)} %get-tuple-element.49) | copy-start | bytes 16
  19.9 55.3 %copy-start.26 = (pred[4]{0:T(512)(128)(4,1)}, pred[4]{0:T(512)(128)(4,1)S(1)}, u32[]{:S(2)}) copy-start(pred[4]{0:T(512)(128)(4,1)S(1)} %get-tuple-element.47) | copy-start | bytes 16
  19.9 92.6 %copy-start.24 = (pred[4]{0:T(512)(128)(4,1)}, pred[4]{0:T(512)(128)(4,1)S(1)}, u32[]{:S(2)}) copy-start(pred[4]{0:T(512)(128)(4,1)S(1)} %get-tuple-element.45) | copy-start | bytes 16
  19.9 146.8 %copy-start.22 = (pred[4]{0:T(512)(128)(4,1)}, pred[4]{0:T(512)(128)(4,1)S(1)}, u32[]{:S(2)}) copy-start(pred[4]{0:T(512)(128)(4,1)S(1)} %get-tuple-element.12) | copy-start | bytes 16
  40.5 18.0 %all-to-all-start.1 = ((bf16[4,2,64,1024]{3,2,1,0:T(8,128)(2,1)}), bf16[4,2,64,1024]{3,2,1,0:T(8,128)(2,1)S(1)}, u32[]{:S(2)}, u32[]{:S(2)}) async-start(bf16[4,2,64,1024]{3,2,1,0:T(8,128)(2,1)} %bitcast.95), calls=%async_computation.2 | async-start | bytes 2097152 | tf_op jit(solution)/shard_map/all_to_all | solution.py:156
  44.0 169.0 %all-gather.8.cloned.1.call-start = ((), (), s32[]{:S(2)}) async-start(), calls=%async_computation.12 | async-start | bytes 2621440 | tf_op jit(solution)/shard_map/all_gather | solution.py:19
  62.1 30.1 %copy-start.4 = (bf16[4,64,1024]{2,1,0:T(8,128)(2,1)}, bf16[4,64,1024]{2,1,0:T(8,128)(2,1)S(1)}, u32[]{:S(2)}) copy-start(bf16[4,64,1024]{2,1,0:T(8,128)(2,1)S(1)} %gather_fusion.1) | copy-start | bytes 1572868
  70.5 18.8 %all-to-all-start.2 = ((bf16[4,2,64,1024]{3,2,1,0:T(8,128)(2,1)}), bf16[4,2,64,1024]{3,2,1,0:T(8,128)(2,1)}, u32[]{:S(2)}, u32[]{:S(2)}) async-start(bf16[4,2,64,1024]{3,2,1,0:T(8,128)(2,1)} %bitcast.93), calls=%async_computation.4 | async-start | bytes 2097152 | tf_op jit(solution)/shard_map/all_to_all | solution.py:156
  74.8 173.4 %all-gather.10.cloned.1.call-start = ((), (), s32[]{:S(2)}) async-start(), calls=%async_computation.14 | async-start | bytes 2621440 | tf_op jit(solution)/shard_map/all_gather | solution.py:19
  94.7 17.8 %copy-start.6 = (bf16[4,64,1024]{2,1,0:T(8,128)(2,1)}, bf16[4,64,1024]{2,1,0:T(8,128)(2,1)S(1)}, u32[]{:S(2)}) copy-start(bf16[4,64,1024]{2,1,0:T(8,128)(2,1)S(1)} %gather_fusion.2) | copy-start | bytes 1572868
  95.7 16.9 %copy-start = (bf16[2,32,1024]{2,1,0:T(8,128)(2,1)S(1)}, bf16[2,32,1024]{2,1,0:T(8,128)(2,1)}, u32[]{:S(2)}) copy-start(bf16[2,32,1024]{2,1,0:T(8,128)(2,1)} %param.13) | copy-start | bytes 393220
  95.7 16.9 %copy-start.21 = (bf16[1,1024]{1,0:T(2,128)(2,1)S(1)}, bf16[1,1024]{1,0:T(2,128)(2,1)}, u32[]{:S(2)}) copy-start(bf16[1,1024]{1,0:T(2,128)(2,1)} %param.17) | copy-start | bytes 6148
  103.2 37.1 %all-to-all-start.3 = ((bf16[4,2,64,1024]{3,2,1,0:T(8,128)(2,1)}), bf16[4,2,64,1024]{3,2,1,0:T(8,128)(2,1)}, u32[]{:S(2)}, u32[]{:S(2)}) async-start(bf16[4,2,64,1024]{3,2,1,0:T(8,128)(2,1)} %bitcast.94), calls=%async_computation.6 | async-start | bytes 2097152 | tf_op jit(solution)/shard_map/all_to_all | solution.py:156
  140.3 34.0 %all-to-all-start.4 = ((bf16[4,2,64,1024]{3,2,1,0:T(8,128)(2,1)}), bf16[4,2,64,1024]{3,2,1,0:T(8,128)(2,1)}, u32[]{:S(2)}, u32[]{:S(2)}) async-start(bf16[4,2,64,1024]{3,2,1,0:T(8,128)(2,1)} %bitcast.92), calls=%async_computation.8 | async-start | bytes 2097152 | tf_op jit(solution)/shard_map/all_to_all | solution.py:156
  144.5 138.9 %all-gather.12.cloned.1.call-start = ((), (), s32[]{:S(2)}) async-start(), calls=%async_computation.16 | async-start | bytes 2621440 | tf_op jit(solution)/shard_map/all_gather | solution.py:19
  152.6 166.2 %all-gather.14.cloned.1.call-start = ((), (), s32[]{:S(2)}) async-start(), calls=%async_computation.18 | async-start | bytes 2621440 | tf_op jit(solution)/shard_map/all_gather | solution.py:19
  152.6 11.7 %slice-start.4 = ((s8[8388608]{0:T(1024)(128)(4,1)}), s8[4194304]{0:T(1024)(128)(4,1)S(1)}, s32[]{:S(2)}) async-start(s8[8388608]{0:T(1024)(128)(4,1)} %bitcast.76), calls=%async_computation.24 | async-start | bytes 8388608
  179.6 10.9 %copy-start.10 = (bf16[4,64,1024]{2,1,0:T(8,128)(2,1)}, bf16[4,64,1024]{2,1,0:T(8,128)(2,1)S(1)}, u32[]{:S(2)}) copy-start(bf16[4,64,1024]{2,1,0:T(8,128)(2,1)S(1)} %gather_fusion.4) | copy-start | bytes 1572868
  180.6 193.0 %reduce-scatter.6.cloned.1.call-start = ((), (), s32[]{:S(2)}) async-start(), calls=%async_computation.11 | async-start | bytes 3932160 | tf_op jit(solution)/shard_map/reduce_scatter | solution.py:36
  180.9 9.6 %slice-start = ((s8[8388608]{0:T(1024)(128)(4,1)}), s8[4194304]{0:T(1024)(128)(4,1)S(1)}, s32[]{:S(2)}) async-start(s8[8388608]{0:T(1024)(128)(4,1)} %bitcast.72), calls=%async_computation.20 | async-start | bytes 8388608
  183.2 10.6 %slice-start.6 = ((s8[8388608]{0:T(1024)(128)(4,1)}), s8[4194304]{0:T(1024)(128)(4,1)S(1)}, s32[]{:S(2)}) async-start(s8[8388608]{0:T(1024)(128)(4,1)} %bitcast.78), calls=%async_computation.26 | async-start | bytes 8388608
  212.5 187.0 %reduce-scatter.8.cloned.1.call-start = ((), (), s32[]{:S(2)}) async-start(), calls=%async_computation.13 | async-start | bytes 3932160 | tf_op jit(solution)/shard_map/reduce_scatter | solution.py:36
  215.1 7.4 %copy-start.13 = (bf16[256,4096]{1,0:T(8,128)(2,1)S(1)}, bf16[256,4096]{1,0:T(8,128)(2,1)}, u32[]{:S(2)}) copy-start(bf16[256,4096]{1,0:T(8,128)(2,1)} %all-gather.8.cloned.1.call-done) | copy-start | bytes 6291460
  215.1 14.2 %slice-start.8 = ((s8[8388608]{0:T(1024)(128)(4,1)}), s8[4194304]{0:T(1024)(128)(4,1)S(1)}, s32[]{:S(2)}) async-start(s8[8388608]{0:T(1024)(128)(4,1)} %bitcast.80), calls=%async_computation.28 | async-start | bytes 8388608
  247.9 214.1 %reduce-scatter.10.cloned.1.call-start = ((), (), s32[]{:S(2)}) async-start(), calls=%async_computation.15 | async-start | bytes 3932160 | tf_op jit(solution)/shard_map/reduce_scatter | solution.py:36
  250.3 14.2 %slice-start.10 = ((s8[8388608]{0:T(1024)(128)(4,1)}), s8[4194304]{0:T(1024)(128)(4,1)S(1)}, s32[]{:S(2)}) async-start(s8[8388608]{0:T(1024)(128)(4,1)} %bitcast.82), calls=%async_computation.30 | async-start | bytes 8388608
  283.2 241.5 %reduce-scatter.12.cloned.1.call-start = ((), (), s32[]{:S(2)}) async-start(), calls=%async_computation.17 | async-start | bytes 3932160 | tf_op jit(solution)/shard_map/reduce_scatter | solution.py:36
  285.6 14.1 %slice-start.2 = ((s8[8388608]{0:T(1024)(128)(4,1)}), s8[4194304]{0:T(1024)(128)(4,1)S(1)}, s32[]{:S(2)}) async-start(s8[8388608]{0:T(1024)(128)(4,1)} %bitcast.74), calls=%async_computation.22 | async-start | bytes 8388608
  318.5 268.7 %reduce-scatter.14.cloned.1.call-start = ((), (), s32[]{:S(2)}) async-start(), calls=%async_computation.19 | async-start | bytes 3932160 | tf_op jit(solution)/shard_map/reduce_scatter | solution.py:36
  320.9 7.5 %copy-start.16 = (bf16[256,4096]{1,0:T(8,128)(2,1)S(1)}, bf16[256,4096]{1,0:T(8,128)(2,1)}, u32[]{:S(2)}) copy-start(bf16[256,4096]{1,0:T(8,128)(2,1)} %all-gather.14.cloned.1.call-done) | copy-start | bytes 6291460
  320.9 14.2 %slice-start.12 = ((s8[8388608]{0:T(1024)(128)(4,1)}), s8[4194304]{0:T(1024)(128)(4,1)S(1)}, s32[]{:S(2)}) async-start(s8[8388608]{0:T(1024)(128)(4,1)} %bitcast.84), calls=%async_computation.32 | async-start | bytes 8388608
  345.3 8.9 %copy-start.32 = (s32[20]{0:T(128)S(1)}, s32[20]{0:T(128)}, u32[]{:S(2)}) copy-start(s32[20]{0:T(128)} %copy-done.31) | copy-start | bytes 244
  345.3 9.6 %copy-start.20 = (s32[20]{0:T(128)S(1)}, s32[20]{0:T(128)}, u32[]{:S(2)}) copy-start(s32[20]{0:T(128)} %copy-done.19) | copy-start | bytes 244
  345.3 10.3 %copy-start.1 = (bf16[2,32,1024]{2,1,0:T(8,128)(2,1)S(1)}, bf16[2,32,1024]{2,1,0:T(8,128)(2,1)}, u32[]{:S(2)}) copy-start(bf16[2,32,1024]{2,1,0:T(8,128)(2,1)} %param.13) | copy-start | bytes 393220
  354.2 15.8 %copy-start.3 = (bf16[4,64,1024]{2,1,0:T(8,128)(2,1)S(1)}, bf16[4,64,1024]{2,1,0:T(8,128)(2,1)}, u32[]{:S(2)}) copy-start(bf16[4,64,1024]{2,1,0:T(8,128)(2,1)} %copy-done.2) | copy-start | bytes 1572868
  354.2 17.4 %copy-start.5 = (bf16[4,64,1024]{2,1,0:T(8,128)(2,1)S(1)}, bf16[4,64,1024]{2,1,0:T(8,128)(2,1)}, u32[]{:S(2)}) copy-start(bf16[4,64,1024]{2,1,0:T(8,128)(2,1)} %copy-done.4) | copy-start | bytes 1572868
  354.2 18.9 %copy-start.7 = (bf16[4,64,1024]{2,1,0:T(8,128)(2,1)S(1)}, bf16[4,64,1024]{2,1,0:T(8,128)(2,1)}, u32[]{:S(2)}) copy-start(bf16[4,64,1024]{2,1,0:T(8,128)(2,1)} %copy-done.6) | copy-start | bytes 1572868
  354.2 18.9 %copy-start.27 = (pred[4]{0:T(512)(128)(4,1)S(1)}, pred[4]{0:T(512)(128)(4,1)}, u32[]{:S(2)}) copy-start(pred[4]{0:T(512)(128)(4,1)} %copy-done.26) | copy-start | bytes 16
  355.6 17.6 %copy-start.9 = (bf16[4,64,1024]{2,1,0:T(8,128)(2,1)S(1)}, bf16[4,64,1024]{2,1,0:T(8,128)(2,1)}, u32[]{:S(2)}) copy-start(bf16[4,64,1024]{2,1,0:T(8,128)(2,1)} %copy-done.8) | copy-start | bytes 1572868
  355.6 17.6 %copy-start.25 = (pred[4]{0:T(512)(128)(4,1)S(1)}, pred[4]{0:T(512)(128)(4,1)}, u32[]{:S(2)}) copy-start(pred[4]{0:T(512)(128)(4,1)} %copy-done.24) | copy-start | bytes 16
  356.8 16.6 %copy-start.11 = (bf16[4,64,1024]{2,1,0:T(8,128)(2,1)S(1)}, bf16[4,64,1024]{2,1,0:T(8,128)(2,1)}, u32[]{:S(2)}) copy-start(bf16[4,64,1024]{2,1,0:T(8,128)(2,1)} %copy-done.10) | copy-start | bytes 1572868
  356.8 16.6 %copy-start.23 = (pred[4]{0:T(512)(128)(4,1)S(1)}, pred[4]{0:T(512)(128)(4,1)}, u32[]{:S(2)}) copy-start(pred[4]{0:T(512)(128)(4,1)} %copy-done.22) | copy-start | bytes 16
  373.3 26.2 %copy-start.17 = (bf16[4,64,1024]{2,1,0:T(8,128)(2,1)S(1)}, bf16[4,64,1024]{2,1,0:T(8,128)(2,1)}, u32[]{:S(2)}) copy-start(bf16[4,64,1024]{2,1,0:T(8,128)(2,1)} %broadcast_select_fusion.9) | copy-start | bytes 1572868
  373.4 151.3 %copy-start.18 = (bf16[4,32,1024]{2,1,0:T(8,128)(2,1)S(1)}, bf16[4,32,1024]{2,1,0:T(8,128)(2,1)}, u32[]{:S(2)}) copy-start(bf16[4,32,1024]{2,1,0:T(8,128)(2,1)} %broadcast_select_fusion.12) | copy-start | bytes 786436
  (14 other events, 84.6 us)
Sparse Core Ops, SparseCore 0:
  35.0 46.9 all-gather.5
  83.6 53.8 all-gather.7
  139.1 44.3 all-gather.9
  184.9 44.6 all-gather.11
  231.0 44.6 all-gather.13
  277.8 58.9 reduce-scatter.5
  339.1 60.2 reduce-scatter.7
  401.7 60.2 reduce-scatter.9
  464.4 60.2 reduce-scatter.11
  526.8 60.2 reduce-scatter.13

commit v2 on v1

--- a/solution.py
+++ b/solution.py
@@ -9,48 +9,8 @@
 PLEN = 64
 GATHER = "native"
 REDUCE = "native"
-CHUNKS = 5
+TENTHS = (3, 7)
 RING_MAX = 8
-
-
-def line_gather(rows, axis):
-    n = lax.axis_size(axis)
-    if GATHER == "native" or n > RING_MAX:
-        return lax.all_gather(rows, axis, axis=1, tiled=True)
-    width = rows.shape[1]
-    from_left, from_right = [], []
-    right, left = rows, rows
-    for step in range(1, n):
-        right = lax.ppermute(right, axis, [(i, i + 1) for i in range(step - 1, n - 1)])
-        left = lax.ppermute(left, axis, [(i, i - 1) for i in range(1, n - step + 1)])
-        from_left.append(right)
-        from_right.append(left)
-    strip = jnp.concatenate(from_left[::-1] + [rows] + from_right, axis=1)
-    me = lax.axis_index(axis)
-    return lax.dynamic_slice_in_dim(strip, (n - 1 - me) * width, n * width, 1)
-
-
-def line_reduce(terms, axis):
-    n = lax.axis_size(axis)
-    if REDUCE == "native" or n > RING_MAX:
-        return lax.psum_scatter(terms, axis, scatter_dimension=1, tiled=True).astype(jnp.float32)
-    width = terms.shape[1] // n
-    me = lax.axis_index(axis)
-
-    def block(index):
-        start = jnp.clip(index, 0, n - 1) * width
-        return lax.dynamic_slice_in_dim(terms, start, width, 1)
-
-    right = left = None
-    for step in range(1, n):
-        reach = n - step
-        out_right, out_left = block(me + reach), block(me - reach)
-        if step > 1:
-            out_right = (out_right.astype(jnp.float32) + right.astype(jnp.float32)).astype(jnp.bfloat16)
-            out_left = (out_left.astype(jnp.float32) + left.astype(jnp.float32)).astype(jnp.bfloat16)
-        right = lax.ppermute(out_right, axis, [(i, i + 1) for i in range(step)])
-        left = lax.ppermute(out_left, axis, [(i, i - 1) for i in range(n - step, n)])
-    return block(me).astype(jnp.float32) + right.astype(jnp.float32) + left.astype(jnp.float32)
 
 
 def attend_kernel(ques_ref, qq, kq, vq, qp, kp, vp, out):
@@ -140,32 +100,35 @@
     source_of, rank_of = in_order(sources), in_order(rank_here)
     question_of = listed // npass
 
-    chunks = CHUNKS if per_reader % CHUNKS == 0 and capacity % CHUNKS == 0 else 1
-    ranks, count = capacity // chunks, per_reader // chunks
-    slot_of = ((rank_of // ranks) * readers + source_of) * ranks + rank_of % ranks
+    split = TENTHS if sum(TENTHS) == capacity and per_reader % capacity == 0 else (capacity,)
+    starts = [sum(split[:c]) for c in range(len(split))]
+    slot_of = jnp.zeros_like(rank_of)
+    for start, ranks in zip(starts, split):
+        slot_of = jnp.where(rank_of >= start, start * readers + source_of * ranks + rank_of - start, slot_of)
 
     question_rows = questions.reshape(q_count * qlen, feat_width)
-    head_rows = line_gather(jnp.concatenate([question_rows, norm_gain], axis=0), "tp")
+    head_rows = lax.all_gather(jnp.concatenate([question_rows, norm_gain], axis=0), "tp", axis=1, tiled=True)
     gain = head_rows[q_count * qlen :]
     ques_qkv = project(normalize(head_rows[: q_count * qlen], gain), weights)
 
     incoming, finished = [], []
-    for c in range(chunks):
-        rows = slot_rows[:, c * ranks : (c + 1) * ranks]
-        picked = jnp.take(memory, rows.reshape(-1), axis=0).reshape(readers, ranks, PLEN, feat_width)
+    for c, (start, ranks) in enumerate(zip(starts, split)):
+        count = ranks * per_reader // capacity
+        rows = slot_rows[:, start : start + ranks]
+        picked = jnp.take(memory, rows.reshape(-1), axis=0, mode="clip").reshape(readers, ranks, PLEN, feat_width)
         arrived = lax.all_to_all(picked, "mem", split_axis=0, concat_axis=0, tiled=True)
         incoming.append(arrived.reshape(readers * ranks, PLEN, feat_width))
-        part = slice(c * count, (c + 1) * count)
+        part = slice(start * per_reader // capacity, (start + ranks) * per_reader // capacity)
         pool = jnp.concatenate(incoming, axis=0) if c else incoming[0]
-        fetched = jnp.take(pool, slot_of[part], axis=0)
-        full = line_gather(fetched.reshape(count * PLEN, feat_width), "tp")
+        fetched = jnp.take(pool, slot_of[part], axis=0, mode="clip")
+        full = lax.all_gather(fetched.reshape(count * PLEN, feat_width), "tp", axis=1, tiled=True)
         pass_qkv = project(normalize(full, gain), weights)
         context = attend(question_of[part], ques_qkv, pass_qkv, qlen)
         terms = jnp.dot(context, w_out, preferred_element_type=jnp.float32).astype(jnp.bfloat16)
-        branch = line_reduce(terms, "tp").reshape(count, qlen + PLEN, feat_width)
-        residual = jnp.concatenate([jnp.take(questions, question_of[part], axis=0), fetched], axis=1)
-        finished.append((residual.astype(jnp.float32) + branch).astype(jnp.bfloat16))
-    mixed = jnp.take(jnp.concatenate(finished, axis=0), place, axis=0)
+        branch = lax.psum_scatter(terms, "tp", scatter_dimension=1, tiled=True).reshape(count, qlen + PLEN, feat_width)
+        residual = jnp.concatenate([jnp.take(questions, question_of[part], axis=0, mode="clip"), fetched], axis=1)
+        finished.append((residual.astype(jnp.float32) + branch.astype(jnp.float32)).astype(jnp.bfloat16))
+    mixed = jnp.take(jnp.concatenate(finished, axis=0), place, axis=0, mode="clip")
     return mixed.reshape(q_count, npass, qlen + PLEN, feat_width)
 
 

time: 616 us -> 536 us (0.87); the launches traced: 606 us -> 533 us
  waiting for transfers between devices: 246 us -> 323 us
  matrix products: 141 us -> 87.9 us
  other arithmetic: 66.9 us -> 23.2 us
  local copies, waits for them, and re-layouts: 57.1 us -> 27.7 us
  starting transfers between devices: 22.1 us -> 9.2 us
  Pallas kernels: 34.1 us -> 26.8 us
    all_gather x5 -> x2, waiting for transfers between devices: 0.09 us -> 64.5 us  [local(): lax.all_gather(fetched.reshape(count * PLEN, feat_width), 'tp', axis=1, t...]
    dot_general x18 -> x9, matrix products: 97 us -> 61 us  [project(): jnp.dot(rows, w, preferred_element_type=jnp.float32).astype(jnp.bfloat16)]
    select_n x27 -> x1, other arithmetic: 29.9 us -> 0.01 us  [local(): jnp.where(rank_of >= start, start * readers + source_of * ranks + rank_of...]
    all_to_all x5 -> x2, waiting for transfers between devices: 41.3 us -> 61.6 us  [local(): lax.all_to_all(picked, 'mem', split_axis=0, concat_axis=0, tiled=True)]
    gather x16 -> x7, local copies, waits for them, and re-layouts: 43.4 us -> 24.4 us  [the longest x2 11.3 us: local(): jnp.take(memory, rows.reshape(-1), axis=0, mode='clip')]
    dot_general x5 -> x2, matrix products: 43.8 us -> 26.9 us  [local(): jnp.dot(context, w_out, preferred_element_type=jnp.float32)]
    all_to_all x5 -> x2, starting transfers between devices: 20.5 us -> 9.08 us  [local(): lax.all_to_all(picked, 'mem', split_axis=0, concat_axis=0, tiled=True)]
    unnamed x11 -> x7, other arithmetic: 9.61 us -> 0.01 us
  transfers between devices with their start and end apart: 15 -> 6, of which waited for: 7 -> 5; matrix products, arithmetic and copies ran while one was open for 40% -> 22% of each run, Pallas kernels for 6% -> 5%
where the time goes in v2:
time: 536 us; the launch traced here: 533 us
  waiting for transfers between devices  323 us (60%)
  matrix products  87.9 us (16%)
  local copies, waits for them, and re-layouts  27.7 us (5%)
  Pallas kernels  26.8 us (5%)
  other arithmetic  23.2 us (4%)
  blocking collectives  21.4 us (4%)
  between operations  13.9 us (3%)
  starting transfers between devices  9.2 us (2%)
    reduce_scatter x2, waiting for transfers between devices, local(): lax.psum_scatter(terms, 'tp', scatter_dimension=1, tiled=True)  196 us
    all_gather x2, waiting for transfers between devices, local(): lax.all_gather(fetched.reshape(count * PLEN, feat_width), 'tp', axis=1, t...  64.5 us
    all_to_all x2, waiting for transfers between devices, local(): lax.all_to_all(picked, 'mem', split_axis=0, concat_axis=0, tiled=True)  61.6 us
    dot_general x9, matrix products, project(): jnp.dot(rows, w, preferred_element_type=jnp.float32).astype(jnp.bfloat16)  61 us
    dot_general x2, matrix products, local(): jnp.dot(context, w_out, preferred_element_type=jnp.float32)  26.9 us
    pallas_call x2, Pallas kernels, attend(): pl.pallas_call(attend_kernel, grid_spec=pltpu.PrefetchScalarGridSpec(num_...  26.8 us
    all_gather x1, blocking collectives, local(): lax.all_gather(jnp.concatenate([question_rows, norm_gain], axis=0), 'tp',...  21.4 us
    gather x2, local copies, waits for them, and re-layouts, local(): jnp.take(memory, rows.reshape(-1), axis=0, mode='clip')  11.3 us
  transfers between devices with their start and end apart: 6, of which 5 were waited for; matrix products, arithmetic and copies ran while one was open for 22% of the time, Pallas kernels for 5%

profile of v2, /device:TPU:0, one launch (start us, length us, event | category | flops | bytes accessed | tf_op | source)
XLA Modules:
  0.0 532.6 jit_solution(5416610157457949798)
XLA Ops:
  6.5 0.8 copy.10
  7.3 1.0 select_reduce_fusion
  8.5 0.4 convert_reduce_fusion
  8.9 0.1 copy.12
  9.0 0.3 select_reduce_fusion.1
  9.3 0.1 copy.13
  9.5 5.2 gather_fusion.1
  14.7 4.2 all-to-all-start
  18.9 0.2 convert_reduce_fusion.2
  19.1 0.2 convert_reduce_fusion.1
  19.3 0.1 select_reduce_fusion.2
  19.4 0.4 copy-done.9
  19.9 19.1 %all-to-all-done = bf16[4,3,64,1024]{3,2,1,0:T(8,128)(2,1)S(1)} async-done(((bf16[4,3,64,1024]{3,2,1,0:T(8,128)(2,1)}), bf16[4,3,64,1024]{3,2,1,0:T(8,128)(2,1)S(1)}, u32[]{:S(2)}, u32[]{:S(2)}) %all-to-all-start) | async-done | bytes 1572896 | tf_op jit(solution)/shard_map/all_to_all | solution.py:119
  39.0 1.5 gather_fusion.2
  40.5 0.1 copy.14
  40.7 6.1 %gather_fusion.4 = bf16[28,64,1024]{2,1,0:T(8,128)(2,1)} fusion(bf16[64,64,1024]{2,1,0:T(8,128)(2,1)} %param.10, s32[1024]{0:T(1024)S(1)} %pad_clamp_fusion.2), kind=kCustom, calls=%fused_computation.4 | custom fusion | bytes 7340144 | tf_op jit(solution)/shard_map/jit(_take)/gather | solution.py:118
  46.8 4.9 all-to-all-start.1
  51.8 42.5 %all-to-all-done.1 = bf16[4,7,64,1024]{3,2,1,0:T(8,128)(2,1)} async-done(((bf16[4,7,64,1024]{3,2,1,0:T(8,128)(2,1)}), bf16[4,7,64,1024]{3,2,1,0:T(8,128)(2,1)}, u32[]{:S(2)}, u32[]{:S(2)}) %all-to-all-start.1) | async-done | bytes 3670048 | tf_op jit(solution)/shard_map/all_to_all | solution.py:119
  94.3 4.8 pad_maximum_fusion
  99.1 4.4 gather_fusion.5
  103.6 0.6 slice.31.ques_ref
  104.3 21.4 %all_gather.9 = bf16[65,4096]{1,0:T(8,128)(2,1)S(1)} all-gather(bf16[65,1024]{1,0:T(8,128)(2,1)S(1)} %pad_maximum_fusion.2), channel_id=1, replica_groups=mesh['groups'=2,'mem'=4,'tp'=4] {'tp'}, dimensions={1}, use_global_device_ids=true | all-gather | bytes 665600 | tf_op jit(solution)/shard_map/all_gather | solution.py:110
  125.7 0.2 fusion.8
  126.0 5.9 %convolution_convert_fusion.8.vq = bf16[64,1024]{1,0:T(8,128)(2,1)} fusion(bf16[4096,1024]{1,0:T(8,128)(2,1)} %param.16, f32[4096]{0:T(1024)S(1)} %bitcast.51, f32[64]{0:T(128)S(1)} %add_rsqrt_fusion.2, bf16[65,4096]{1,0:T(8,128)(2,1)S(1)} %all_gather.9), kind=kOutput, calls=%fused_computation.33 | convolution fusion | flops 537985024 | bytes 9060864 | tf_op jit(solution)/shard_map/dot_general | solution.py:64
  131.9 2.3 convolution_convert_fusion.9.kq
  134.2 2.3 convolution_convert_fusion.10.qq
  136.5 2.8 fusion.3
  139.3 8.9 %convolution_convert_fusion.5.vp = bf16[384,1024]{1,0:T(8,128)(2,1)} fusion(bf16[4096,1024]{1,0:T(8,128)(2,1)} %param.16, bf16[384,4096]{1,0:T(8,128)(2,1)} %all-gather.3.cloned.1.call-done, f32[4096]{0:T(1024)S(1)} %bitcast.54, f32[384]{0:T(512)S(1)} %add_rsqrt_fusion.1), kind=kOutput, calls=%fused_computation.28 | convolution fusion | flops 3227910144 | bytes 12338688 | tf_op jit(solution)/shard_map/dot_general | solution.py:64
  148.3 4.4 convolution_convert_fusion.6.kp
  152.7 4.4 convolution_convert_fusion.7.qp
  157.1 9.1 %shard_map.91 = bf16[576,1024]{1,0:T(8,128)(2,1)} custom-call(s32[6]{0:T(128)} %bitcast.61, bf16[64,1024]{1,0:T(8,128)(2,1)} %convolution_convert_fusion.10.qq, bf16[64,1024]{1,0:T(8,128)(2,1)} %convolution_convert_fusion.9.kq, bf16[64,1024]{1,0:T(8,128)(2,1)} %convolution_convert_fusion.8.vq, bf16[384,1024]{1,0:T(8,128)(2,1)} %convolution_convert_fusion.7.qp, ...), custom_call_target="tpu_custom_call" | custom-call | flops 452984832 | bytes 4718592 | tf_op jit(solution)/shard_map/pallas_call | solution.py:40
  166.2 9.3 %convolution_convert_fusion.1 = bf16[576,4096]{1,0:T(8,128)(2,1)} fusion(bf16[576,1024]{1,0:T(8,128)(2,1)} %shard_map.91, bf16[1024,4096]{1,0:T(8,128)(2,1)} %param.17), kind=kOutput, calls=%fused_computation.18 | convolution fusion | flops 4834197504 | bytes 14286848 | tf_op jit(solution)/shard_map/dot_general | solution.py:127
  175.6 64.5 %all-gather.5.cloned.1.call-done = bf16[896,4096]{1,0:T(8,128)(2,1)} async-done(((bf16[896,1024]{1,0:T(8,128)(2,1)}), bf16[896,4096]{1,0:T(8,128)(2,1)}) %all-gather.5.cloned.1.call-update) | async-done | bytes 7340048 | tf_op jit(solution)/shard_map/all_gather | solution.py:124
  240.1 4.7 fusion
  244.8 14.4 %convolution_convert_fusion.2.vp = bf16[896,1024]{1,0:T(8,128)(2,1)} fusion(bf16[4096,1024]{1,0:T(8,128)(2,1)} %param.16, bf16[896,4096]{1,0:T(8,128)(2,1)} %all-gather.5.cloned.1.call-done, f32[4096]{0:T(1024)S(1)} %bitcast.57, f32[896]{0:T(1024)S(1)} %add_rsqrt_fusion), kind=kOutput, calls=%fused_computation.25 | convolution fusion | flops 7531790336 | bytes 17583616 | tf_op jit(solution)/shard_map/dot_general | solution.py:64
  259.2 9.2 %convolution_convert_fusion.3.kp = bf16[896,1024]{1,0:T(8,128)(2,1)} fusion(bf16[4096,1024]{1,0:T(8,128)(2,1)S(1)} %bitcast.35, bf16[896,4096]{1,0:T(8,128)(2,1)S(1)} %bitcast.48, f32[4096]{0:T(1024)S(1)} %bitcast.58, f32[896]{0:T(1024)S(1)} %add_rsqrt_fusion), kind=kOutput, calls=%fused_computation.26 | convolution fusion | flops 7531790336 | bytes 17583616 | tf_op jit(solution)/shard_map/dot_general | solution.py:64
  268.5 9.3 %convolution_convert_fusion.4.qp = bf16[896,1024]{1,0:T(8,128)(2,1)} fusion(bf16[4096,1024]{1,0:T(8,128)(2,1)S(1)} %bitcast.41, bf16[896,4096]{1,0:T(8,128)(2,1)S(1)} %bitcast.48, f32[4096]{0:T(1024)S(1)} %bitcast.59, f32[896]{0:T(1024)S(1)} %add_rsqrt_fusion), kind=kOutput, calls=%fused_computation.27 | convolution fusion | flops 7531790336 | bytes 17583616 | tf_op jit(solution)/shard_map/dot_general | solution.py:64
  277.7 17.7 %shard_map.92 = bf16[1344,1024]{1,0:T(8,128)(2,1)} custom-call(s32[14]{0:T(128)} %slice.31.ques_ref, bf16[64,1024]{1,0:T(8,128)(2,1)} %convolution_convert_fusion.10.qq, bf16[64,1024]{1,0:T(8,128)(2,1)} %convolution_convert_fusion.9.kq, bf16[64,1024]{1,0:T(8,128)(2,1)} %convolution_convert_fusion.8.vq, bf16[896,1024]{1,0:T(8,128)(2,1)} %convolution_convert_fusion.4.qp, ...), custom_call_target="tpu_custom_call" | custom-call | flops 1056964608 | bytes 11010048 | tf_op jit(solution)/shard_map/pallas_call | solution.py:40
  295.4 17.6 %convolution_convert_fusion = bf16[1344,4096]{1,0:T(8,128)(2,1)} fusion(bf16[1344,1024]{1,0:T(8,128)(2,1)} %shard_map.92, bf16[1024,4096]{1,0:T(8,128)(2,1)} %param.17), kind=kOutput, calls=%fused_computation.9 | convolution fusion | flops 11279794176 | bytes 22151168 | tf_op jit(solution)/shard_map/dot_general | solution.py:127
  313.0 0.6 copy-done.8
  313.7 1.6 gather_fusion.3
  315.2 0.6 gather_fusion
  315.8 10.0 %reduce-scatter.3.cloned.1.call-done = bf16[576,1024]{1,0:T(8,128)(2,1)} async-done(((bf16[576,4096]{1,0:T(8,128)(2,1)}), bf16[576,1024]{1,0:T(8,128)(2,1)}) %reduce-scatter.3.cloned.1.call-update) | async-done | bytes 1179664 | tf_op jit(solution)/shard_map/reduce_scatter | solution.py:128
  325.8 2.8 fusion.7
  328.6 186.5 %reduce-scatter.5.cloned.1.call-done = bf16[1344,1024]{1,0:T(8,128)(2,1)} async-done(((bf16[1344,4096]{1,0:T(8,128)(2,1)}), bf16[1344,1024]{1,0:T(8,128)(2,1)}) %reduce-scatter.5.cloned.1.call-update) | async-done | bytes 2752528 | tf_op jit(solution)/shard_map/reduce_scatter | solution.py:128
  515.0 3.4 fusion.6
  518.4 2.2 pad_maximum_fusion.1
  520.6 5.1 gather_fusion.6
  (90 shorter events, 0.9 us)
Async XLA Ops:
  14.7 24.3 %all-to-all-start = ((bf16[4,3,64,1024]{3,2,1,0:T(8,128)(2,1)}), bf16[4,3,64,1024]{3,2,1,0:T(8,128)(2,1)S(1)}, u32[]{:S(2)}, u32[]{:S(2)}) async-start(bf16[4,3,64,1024]{3,2,1,0:T(8,128)(2,1)} %bitcast.1), calls=%async_computation | async-start | bytes 3145728 | tf_op jit(solution)/shard_map/all_to_all | solution.py:119
  18.9 117.6 %all-gather.3.cloned.1.call-start = ((), (), s32[]{:S(2)}) async-start(), calls=%async_computation.4 | async-start | bytes 3932160 | tf_op jit(solution)/shard_map/all_gather | solution.py:124
  19.3 0.6 copy-start.9
  46.8 47.5 %all-to-all-start.1 = ((bf16[4,7,64,1024]{3,2,1,0:T(8,128)(2,1)}), bf16[4,7,64,1024]{3,2,1,0:T(8,128)(2,1)}, u32[]{:S(2)}, u32[]{:S(2)}) async-start(bf16[4,7,64,1024]{3,2,1,0:T(8,128)(2,1)} %bitcast.44), calls=%async_computation.2 | async-start | bytes 7340032 | tf_op jit(solution)/shard_map/all_to_all | solution.py:119
  51.6 188.4 %all-gather.5.cloned.1.call-start = ((), (), s32[]{:S(2)}) async-start(), calls=%async_computation.6 | async-start | bytes 9175040 | tf_op jit(solution)/shard_map/all_gather | solution.py:124
  94.3 10.0 %copy-start.1 = (bf16[2,32,1024]{2,1,0:T(8,128)(2,1)S(1)}, bf16[2,32,1024]{2,1,0:T(8,128)(2,1)}, u32[]{:S(2)}) copy-start(bf16[2,32,1024]{2,1,0:T(8,128)(2,1)} %param.9) | copy-start | bytes 393220
  94.3 10.0 %copy-start.5 = (bf16[1,1024]{1,0:T(2,128)(2,1)S(1)}, bf16[1,1024]{1,0:T(2,128)(2,1)}, u32[]{:S(2)}) copy-start(bf16[1,1024]{1,0:T(2,128)(2,1)} %param.13) | copy-start | bytes 6148
  103.6 222.2 %reduce-scatter.3.cloned.1.call-start = ((), (), s32[]{:S(2)}) async-start(), calls=%async_computation.5 | async-start | bytes 5898240 | tf_op jit(solution)/shard_map/reduce_scatter | solution.py:128
  103.6 28.2 %copy-start.6 = (s32[20]{0:T(128)}, s32[20]{0:T(128)S(1)}, u32[]{:S(2)}) copy-start(s32[20]{0:T(128)S(1)} %and_select_fusion) | copy-start | bytes 244
  104.3 27.6 %slice-start = ((s8[8388608]{0:T(1024)(128)(4,1)}), s8[4194304]{0:T(1024)(128)(4,1)S(1)}, s32[]{:S(2)}) async-start(s8[8388608]{0:T(1024)(128)(4,1)} %bitcast.30), calls=%async_computation.8 | async-start | bytes 8388608
  125.9 5.9 %slice-start.1 = ((s8[8388608]{0:T(1024)(128)(4,1)}), s8[4194304]{0:T(1024)(128)(4,1)S(1)}, s32[]{:S(2)}) async-start(s8[8388608]{0:T(1024)(128)(4,1)} %bitcast.30), calls=%async_computation.9 | async-start | bytes 8388608
  126.0 8.3 %slice-start.6 = ((s8[8388608]{0:T(1024)(128)(4,1)}), s8[4194304]{0:T(1024)(128)(4,1)S(1)}, s32[]{:S(2)}) async-start(s8[8388608]{0:T(1024)(128)(4,1)} %bitcast.36), calls=%async_computation.14 | async-start | bytes 8388608
  131.9 2.3 slice-start.7
  136.5 11.7 %slice-start.2 = ((s8[8388608]{0:T(1024)(128)(4,1)}), s8[4194304]{0:T(1024)(128)(4,1)S(1)}, s32[]{:S(2)}) async-start(s8[8388608]{0:T(1024)(128)(4,1)} %bitcast.32), calls=%async_computation.10 | async-start | bytes 8388608
  139.3 8.9 %slice-start.3 = ((s8[8388608]{0:T(1024)(128)(4,1)}), s8[4194304]{0:T(1024)(128)(4,1)S(1)}, s32[]{:S(2)}) async-start(s8[8388608]{0:T(1024)(128)(4,1)} %bitcast.32), calls=%async_computation.11 | async-start | bytes 8388608
  139.3 8.9 %copy-start.4 = (bf16[384,4096]{1,0:T(8,128)(2,1)S(1)}, bf16[384,4096]{1,0:T(8,128)(2,1)}, u32[]{:S(2)}) copy-start(bf16[384,4096]{1,0:T(8,128)(2,1)} %all-gather.3.cloned.1.call-done) | copy-start | bytes 9437188
  139.3 13.3 %slice-start.8 = ((s8[8388608]{0:T(1024)(128)(4,1)}), s8[4194304]{0:T(1024)(128)(4,1)S(1)}, s32[]{:S(2)}) async-start(s8[8388608]{0:T(1024)(128)(4,1)} %bitcast.38), calls=%async_computation.16 | async-start | bytes 8388608
  148.2 4.4 slice-start.9
  175.5 339.5 %reduce-scatter.5.cloned.1.call-start = ((), (), s32[]{:S(2)}) async-start(), calls=%async_computation.7 | async-start | bytes 13762560 | tf_op jit(solution)/shard_map/reduce_scatter | solution.py:128
  240.1 19.1 %slice-start.4 = ((s8[8388608]{0:T(1024)(128)(4,1)}), s8[4194304]{0:T(1024)(128)(4,1)S(1)}, s32[]{:S(2)}) async-start(s8[8388608]{0:T(1024)(128)(4,1)} %bitcast.34), calls=%async_computation.12 | async-start | bytes 8388608
  240.1 19.1 %slice-start.12 = ((s8[7340032]{0:T(1024)(128)(4,1)}), s8[4194304]{0:T(1024)(128)(4,1)S(1)}, s32[]{:S(2)}) async-start(s8[7340032]{0:T(1024)(128)(4,1)} %bitcast.47), calls=%async_computation.20 | async-start | bytes 8388608
  244.8 14.4 %slice-start.5 = ((s8[8388608]{0:T(1024)(128)(4,1)}), s8[4194304]{0:T(1024)(128)(4,1)S(1)}, s32[]{:S(2)}) async-start(s8[8388608]{0:T(1024)(128)(4,1)} %bitcast.34), calls=%async_computation.13 | async-start | bytes 8388608
  244.8 14.4 %slice-start.13 = ((s8[7340032]{0:T(1024)(128)(4,1)}), s8[3145728]{0:T(1024)(128)(4,1)S(1)}, s32[]{:S(2)}) async-start(s8[7340032]{0:T(1024)(128)(4,1)} %bitcast.47), calls=%async_computation.21 | async-start | bytes 6291456
  244.8 23.6 %slice-start.10 = ((s8[8388608]{0:T(1024)(128)(4,1)}), s8[4194304]{0:T(1024)(128)(4,1)S(1)}, s32[]{:S(2)}) async-start(s8[8388608]{0:T(1024)(128)(4,1)} %bitcast.40), calls=%async_computation.18 | async-start | bytes 8388608
  259.2 9.2 %slice-start.11 = ((s8[8388608]{0:T(1024)(128)(4,1)}), s8[4194304]{0:T(1024)(128)(4,1)S(1)}, s32[]{:S(2)}) async-start(s8[8388608]{0:T(1024)(128)(4,1)} %bitcast.40), calls=%async_computation.19 | async-start | bytes 8388608
  313.0 0.7 copy-start.8
  313.0 2.2 copy-start.7
  313.0 2.8 copy-start.10
  313.0 12.8 %copy-start.2 = (bf16[6,64,1024]{2,1,0:T(8,128)(2,1)S(1)}, bf16[6,64,1024]{2,1,0:T(8,128)(2,1)}, u32[]{:S(2)}) copy-start(bf16[6,64,1024]{2,1,0:T(8,128)(2,1)} %gather_fusion.2) | copy-start | bytes 2359300
  313.6 201.4 %copy-start = (bf16[14,64,1024]{2,1,0:T(8,128)(2,1)S(1)}, bf16[14,64,1024]{2,1,0:T(8,128)(2,1)}, u32[]{:S(2)}) copy-start(bf16[14,64,1024]{2,1,0:T(8,128)(2,1)} %gather_fusion.5) | copy-start | bytes 5505028
  328.6 189.8 %copy-start.3 = (bf16[6,96,1024]{2,1,0:T(8,128)(2,1)S(1)}, bf16[6,96,1024]{2,1,0:T(8,128)(2,1)}, u32[]{:S(2)}) copy-start(bf16[6,96,1024]{2,1,0:T(8,128)(2,1)} %fusion.7) | copy-start | bytes 3538948
Sparse Core Ops, SparseCore 0:
  40.6 64.5 all-gather.2
  106.8 133.2 all-gather.4
  242.4 83.3 reduce-scatter.2
  328.0 186.9 reduce-scatter.4
